TPU v7x, 32 devices: a whole 2x2x4 slice. The times are simulated.
32 devices in a mesh: heads: 4 (over y, x), seq: 8 (over z, core).
Axes of the slice: x: 2, y: 2, z: 4, core: 2. Of those that a mesh axis runs over, the one named last changes fastest.
Arguments:
- hidden: bfloat16 [64, 2048], P(None, 'seq')
- w_qkv: bfloat16 [2048, 3, 2048], P('seq', None, 'heads')
- w_out: bfloat16 [2048, 2048], P('heads', 'seq'), may hold values from -0.125 to 0.125
- positions: int32 [64], replicated, may hold values from 0 to 8191
- req_blocks: int32 [64], replicated, may hold values from 1 to 64, 144 in all
- keep_list: int32 [144], P('seq'), may hold values from 0 to 1, as said below
- dest_slot: int32 [144], P('seq'), may hold values from 0 to 127, as said below
- key_cache: bfloat16 [144, 128, 2048], P('seq', None, 'heads')
- value_cache: bfloat16 [144, 128, 2048], P('seq', None, 'heads')
- fold_weight: float32 [144, 128], P('seq'), may hold values from 0.1 to 10
Outputs:
- packed_keys: bfloat16 [128, 128, 2048], P('seq', None, 'heads')
- packed_values: bfloat16 [128, 128, 2048], P('seq', None, 'heads')
- packed_request: int32 [128], P('seq')
- folded_keys: bfloat16 [144, 2048], P('seq', 'heads')
- folded_values: bfloat16 [144, 2048], P('seq', 'heads')
- attn_out: bfloat16 [64, 2048], P(None, 'seq')
Inputs may be any that keep to these rules, and one draw needn't show every extreme that they name: `keep_list`: each index of seq (its 18 blocks) keeps at most 15 blocks, and some index keeps exactly that many. `dest_slot`: for a kept block: its slot among 128 packed slots, 16 to each owner (owner = slot // 16); kept blocks have distinct slots; a kept block held by index i of seq goes to owner (i + j) mod 8 for some j with 0 <= j < 4; at most 4 kept blocks of one index share an owner, and some index sends that many to one owner; some owner has all its slots filled. Entries of dropped blocks are meaningless.
All inputs are finite; a program needn't handle non-finite values.
Results may differ from a plain program's by a relative error of at most 0.0156.
The roundings to bfloat16 on the way count: a program that leaves them out, or rounds other values in their place, can miss the bound.
Values may be sent and summed in bfloat16 or wider, within the bound.
A program may use at most 128 MiB of HBM per device.

v0:
```python
import math

import jax
import jax.numpy as jnp
from jax import lax
from jax.sharding import PartitionSpec as P

D = 2048
HDIM = 64
ROWS = 128
HOPS = 4
CAP = 4
SLOT_DEV = 16


ROPE_BASE = 130000.0
NORM_EPSILON = 1e-05
MASKED_SCORE = -1e30


def passed_along(array, axis, by):
    count = lax.axis_size(axis)
    return lax.ppermute(array, axis, [(i, (i + by) % count) for i in range(count)])


def rotate_half(values, cos_table, sin_table):
    half = values.shape[-1] // 2
    lower = values[..., :half]
    upper = values[..., half:]
    return jnp.concatenate(
        [lower * cos_table - upper * sin_table, upper * cos_table + lower * sin_table], axis=-1
    )


def rope_tables(positions, head_size):
    half = head_size // 2
    freqs = ROPE_BASE ** (-(2.0 * jnp.arange(half, dtype=jnp.float32)) / head_size)
    angles = positions.astype(jnp.float32)[:, None] * freqs[None, :]
    return (jnp.cos(angles)[:, None, :], jnp.sin(angles)[:, None, :])


def shards(
    hidden,
    w_qkv,
    w_out,
    positions,
    req_blocks,
    keep_list,
    dest_slot,
    key_cache,
    value_cache,
    fold_weight,
):
    requests = hidden.shape[0]
    n_blocks, row_count, feat_width = key_cache.shape
    heads_here = feat_width // HDIM
    seq_count = lax.axis_size("seq")
    my_index = lax.axis_index("seq")
    widened = hidden.astype(jnp.float32)
    total_sq = lax.psum(jnp.sum(widened * widened, axis=1), "seq")
    normed = (widened * lax.rsqrt(total_sq / D + NORM_EPSILON)[:, None]).astype(jnp.bfloat16)
    partial_value = jnp.dot(
        normed, w_qkv.reshape(w_qkv.shape[0], 3 * feat_width), preferred_element_type=jnp.float32
    )
    proj_all = lax.psum(partial_value, "seq").reshape(requests, 3, heads_here, HDIM)
    cos_table, sin_table = rope_tables(positions, HDIM)
    queries = rotate_half(proj_all[:, 0], cos_table, sin_table).astype(jnp.bfloat16)
    new_keys = rotate_half(proj_all[:, 1], cos_table, sin_table).astype(jnp.bfloat16)
    new_values = proj_all[:, 2].astype(jnp.bfloat16)
    block_ids = jnp.arange(n_blocks, dtype=jnp.int32)
    global_ids = my_index * n_blocks + block_ids
    req_ends = jnp.cumsum(req_blocks)
    blk_req = jnp.sum((global_ids[:, None] >= req_ends[None, :]).astype(jnp.int32), axis=1)
    is_kept = keep_list == 1
    weight_sum = jnp.sum(fold_weight, axis=1)
    fold_keys = jnp.einsum(
        "bi,bif->bf",
        fold_weight,
        key_cache,
        preferred_element_type=jnp.float32,
        precision=lax.Precision.HIGHEST,
    )
    fold_values = jnp.einsum(
        "bi,bif->bf",
        fold_weight,
        value_cache,
        preferred_element_type=jnp.float32,
        precision=lax.Precision.HIGHEST,
    )
    folded_keys = jnp.where(is_kept[:, None], 0.0, fold_keys / weight_sum[:, None]).astype(
        jnp.bfloat16
    )
    folded_values = jnp.where(is_kept[:, None], 0.0, fold_values / weight_sum[:, None]).astype(
        jnp.bfloat16
    )
    owners = dest_slot // SLOT_DEV
    local_slot = dest_slot % SLOT_DEV
    hop_of = (owners - my_index) % seq_count
    earlier = (
        is_kept[None, :]
        & is_kept[:, None]
        & (hop_of[None, :] == hop_of[:, None])
        & (block_ids[None, :] < block_ids[:, None])
    )
    placed = jnp.sum(earlier.astype(jnp.int32), axis=1)
    arrivals = HOPS * CAP
    send_pos = jnp.where(is_kept, hop_of * CAP + placed, arrivals)
    targets = jnp.arange(arrivals, dtype=jnp.int32)
    hit_table = send_pos[None, :] == targets[:, None]
    has_block = jnp.any(hit_table, axis=1)
    source = jnp.sum(jnp.where(hit_table, block_ids[None, :], 0), axis=1)
    send_keys = jnp.where(
        has_block[:, None, None], key_cache[source], jnp.zeros((), jnp.bfloat16)
    ).reshape(HOPS, CAP, row_count, feat_width)
    send_values = jnp.where(
        has_block[:, None, None], value_cache[source], jnp.zeros((), jnp.bfloat16)
    ).reshape(HOPS, CAP, row_count, feat_width)
    meta_data = jnp.stack(
        [jnp.where(has_block, local_slot[source], -1), jnp.where(has_block, blk_req[source], -1)],
        axis=-1,
    )
    meta_data = meta_data.astype(jnp.float32).astype(jnp.bfloat16).reshape(HOPS, CAP, 2)
    arrived = [(send_keys[0], send_values[0], meta_data[0])]
    for distance in range(1, HOPS):
        arrived.append(
            passed_along(
                (send_keys[distance], send_values[distance], meta_data[distance]), "seq", distance
            )
        )
    recv_keys = jnp.stack([entry[0] for entry in arrived])
    recv_values = jnp.stack([entry[1] for entry in arrived])
    recv_meta = jnp.stack([entry[2] for entry in arrived])
    recv_keys = recv_keys.reshape(arrivals, row_count, feat_width)
    recv_values = recv_values.reshape(arrivals, row_count, feat_width)
    recv_meta = recv_meta.reshape(arrivals, 2).astype(jnp.float32).astype(jnp.int32)
    match_table = recv_meta[None, :, 0] == jnp.arange(SLOT_DEV, dtype=jnp.int32)[:, None]
    filled = jnp.any(match_table, axis=1)
    picked = jnp.sum(
        jnp.where(match_table, jnp.arange(arrivals, dtype=jnp.int32)[None, :], 0), axis=1
    )
    packed_keys = jnp.where(filled[:, None, None], recv_keys[picked], jnp.zeros((), jnp.bfloat16))
    packed_values = jnp.where(
        filled[:, None, None], recv_values[picked], jnp.zeros((), jnp.bfloat16)
    )
    packed_request = jnp.where(filled, recv_meta[picked, 1], -1)
    row_keys = packed_keys.reshape(-1, heads_here, HDIM)
    row_values = packed_values.reshape(-1, heads_here, HDIM)
    row_req = jnp.repeat(packed_request, row_count)
    all_keys = jnp.concatenate([row_keys, folded_keys.reshape(n_blocks, heads_here, HDIM)], axis=0)
    all_values = jnp.concatenate(
        [row_values, folded_values.reshape(n_blocks, heads_here, HDIM)], axis=0
    )
    all_req = jnp.concatenate([row_req, jnp.where(is_kept, -1, blk_req)])
    bias = jnp.concatenate(
        [
            jnp.zeros((row_req.shape[0],), jnp.float32),
            jnp.full((n_blocks,), math.log(ROWS), jnp.float32),
        ]
    )
    row_mask = all_req[None, :] == jnp.arange(requests, dtype=jnp.int32)[:, None]
    scores = (
        jnp.einsum("rhd,nhd->hrn", queries, all_keys, preferred_element_type=jnp.float32) * 0.125
        + bias[None, None, :]
    )
    scores = jnp.where(row_mask[None], scores, MASKED_SCORE)
    local_top = jnp.max(scores, axis=2)
    expo = jnp.where(row_mask[None], jnp.exp(scores - local_top[..., None]), 0.0)
    local_sum = jnp.sum(expo, axis=2)
    local_acc = jnp.einsum(
        "hrn,nhd->hrd", expo.astype(jnp.bfloat16), all_values, preferred_element_type=jnp.float32
    )
    top_score = lax.pmax(local_top, "seq")
    factor = jnp.exp(local_top - top_score)
    totals, mixture = lax.psum((local_sum * factor, local_acc * factor[..., None]), "seq")
    own_score = (
        jnp.einsum("rhd,rhd->hr", queries, new_keys, preferred_element_type=jnp.float32) * 0.125
    )
    final_top = jnp.maximum(top_score, own_score)
    shrink = jnp.exp(top_score - final_top)
    own_expo = jnp.exp(own_score - final_top)
    own_prob = lax.optimization_barrier(own_expo.astype(jnp.bfloat16)).astype(jnp.float32)
    totals = totals * shrink + own_expo
    own_values = jnp.transpose(new_values, (1, 0, 2)).astype(jnp.float32)
    mixture = mixture * shrink[..., None] + own_prob[..., None] * own_values
    mixed = (mixture / totals[..., None]).astype(jnp.bfloat16)
    mixed_rows = jnp.transpose(mixed, (1, 0, 2)).reshape(requests, feat_width)
    out_terms = jnp.dot(mixed_rows, w_out, preferred_element_type=jnp.float32)
    attn_out = lax.psum(out_terms, "heads").astype(jnp.bfloat16)
    return (packed_keys, packed_values, packed_request, folded_keys, folded_values, attn_out)


def solution(mesh):
    return jax.shard_map(
        shards,
        mesh=mesh,
        in_specs=(
            P(None, "seq"),
            P("seq", None, "heads"),
            P("heads", "seq"),
            P(),
            P(),
            P("seq"),
            P("seq"),
            P("seq", None, "heads"),
            P("seq", None, "heads"),
            P("seq", None),
        ),
        out_specs=(
            P("seq", None, "heads"),
            P("seq", None, "heads"),
            P("seq"),
            P("seq", "heads"),
            P("seq", "heads"),
            P(None, "seq"),
        ),
        check_vma=False,
    )
```

profile of v0, /device:TPU:0, one launch (start us, length us, event | category | flops | bytes accessed | tf_op | source)
XLA Modules:
  0.0 314.2 jit_solution(5172325780745706765)
XLA Ops:
  13.5 2.5 collective-permute-start.2
  16.0 1.6 collective-permute-start.1
  17.6 1.4 collective-permute-start
  19.8 15.7 %psum.35 = f32[64]{0:T(128)S(1)} all-reduce(f32[64]{0:T(128)S(1)} %fusion.27), channel_id=1, replica_groups=mesh['heads'=4,'seq'=8] {'seq'}, use_global_device_ids=true, to_apply=%region_9.10 | all-reduce | flops 64 | bytes 512 | tf_op jit(solution)/shard_map/psum | solution.py:60
  35.6 1.4 copy.46
  39.4 3.7 %gather_fusion.4 = bf16[16,128,512]{2,1,0:T(8,128)(2,1)} fusion(bf16[18,128,512]{2,1,0:T(8,128)(2,1)} %param.18, s32[1024]{0:T(1024)S(1)} %pad_clamp_fusion.1), kind=kCustom, calls=%fused_computation.4 | custom fusion | bytes 4194368 | tf_op jit(solution)/shard_map/gather | solution.py:116
  43.0 2.0 gather_fusion.2
  45.0 3.9 %broadcast_select_fusion = (bf16[16,128,512]{2,1,0:T(8,128)(2,1)S(1)}, bf16[16,128,512]{2,1,0:T(8,128)(2,1)}) fusion(bf16[16,128,512]{2,1,0:T(8,128)(2,1)} %gather_fusion.4, pred[16]{0:T(512)(128)(4,1)S(1)} %fusion.38, bf16[16,128,512]{2,1,0:T(8,128)(2,1)} %gather_fusion.2), kind=kLoop, calls=%fused_computation.25 | loop fusion | flops 2097152 | bytes 8388624 | tf_op jit(solution)/shard_map/jit(_where)/select_n | solution.py:115
  54.7 2.7 slice_bitcast_fusion.1
  58.9 2.3 collective-permute-start.5
  61.9 1.7 collective-permute-start.4
  66.5 1.3 pad_clamp_fusion
  67.8 45.1 %collective-permute-done.8 = bf16[4,128,512]{2,1,0:T(8,128)(2,1)} collective-permute-done((bf16[4,128,512]{2,1,0:T(8,128)(2,1)}, bf16[4,128,512]{2,1,0:T(8,128)(2,1)}, u32[]{:S(2)}, u32[]{:S(2)}) %collective-permute-start.8) | collective-permute-done | bytes 524320 | tf_op jit(solution)/shard_map/ppermute | solution.py:23
  112.9 41.4 %all-reduce.4.cloned.1.call-done = f32[64,3,8,64]{3,0,2,1:T(8,128)} async-done(((f32[64,3,8,64]{3,0,2,1:T(8,128)}), f32[64,3,8,64]{3,0,2,1:T(8,128)}) %all-reduce.4.cloned.1.call-update) | async-done | bytes 393232 | tf_op jit(solution)/shard_map/psum | solution.py:65
  157.3 2.9 pad_maximum_fusion.1
  160.3 3.7 %gather_fusion.5 = bf16[16,128,512]{2,1,0:T(8,128)(2,1)} fusion(bf16[16,128,512]{2,1,0:T(8,128)(2,1)} %bitcast.101, s32[1024]{0:T(1024)} %pad_clamp_fusion), kind=kCustom, calls=%fused_computation.5 | custom fusion | bytes 4194368 | tf_op jit(solution)/shard_map/gather | solution.py:143
  164.0 4.5 %copy.50 = bf16[16,128,512]{1,0,2:T(8,128)(2,1)} copy(bf16[16,128,512]{2,1,0:T(8,128)(2,1)} %gather_fusion.5) | data formatting | bytes 4194304 | tf_op jit(solution)/shard_map/gather | solution.py:143
  168.5 2.9 pad_maximum_fusion
  171.4 3.7 %gather_fusion.3 = bf16[16,128,512]{2,1,0:T(8,128)(2,1)} fusion(bf16[16,128,512]{2,1,0:T(8,128)(2,1)} %bitcast.100, s32[1024]{0:T(1024)} %pad_clamp_fusion), kind=kCustom, calls=%fused_computation.3 | custom fusion | bytes 4194368 | tf_op jit(solution)/shard_map/gather | solution.py:141
  175.2 4.6 %broadcast_select_fusion.2 = (bf16[16,128,512]{2,1,0:T(8,128)(2,1)}, bf16[16,128,512]{2,1,0:T(8,128)(2,1)}) fusion(bf16[16,128,512]{2,1,0:T(8,128)(2,1)} %gather_fusion.5, pred[16]{0:T(512)(128)(4,1)S(1)} %copy-done.13, bf16[16,128,512]{2,1,0:T(8,128)(2,1)} %gather_fusion.3), kind=kLoop, calls=%fused_computation.27 | loop fusion | flops 2097152 | bytes 8388624 | tf_op jit(solution)/shard_map/jit(_where)/select_n | solution.py:142
  179.7 4.5 %copy.48 = bf16[16,128,512]{1,0,2:T(8,128)(2,1)} copy(bf16[16,128,512]{2,1,0:T(8,128)(2,1)} %gather_fusion.3) | data formatting | bytes 4194304 | tf_op jit(solution)/shard_map/gather | solution.py:141
  184.3 4.2 %gather.33 = bf16[2048,8,64]{0,2,1:T(8,128)(2,1)} reshape(bf16[16,128,512]{1,0,2:T(8,128)(2,1)} %copy.50) | data formatting | bytes 4194304 | tf_op jit(solution)/shard_map/gather | solution.py:143
  188.4 4.2 %gather.32 = bf16[2048,8,64]{0,2,1:T(8,128)(2,1)} reshape(bf16[16,128,512]{1,0,2:T(8,128)(2,1)} %copy.48) | data formatting | bytes 4194304 | tf_op jit(solution)/shard_map/gather | solution.py:141
  192.6 3.9 %broadcast_select_fusion.4 = (bf16[2048,8,64]{0,2,1:T(8,128)(2,1)}, bf16[2048,8,64]{0,2,1:T(8,128)(2,1)S(1)}) fusion(bf16[2048,8,64]{0,2,1:T(8,128)(2,1)} %gather.33, pred[2048]{0:T(1024)(128)(4,1)S(1)} %broadcast_bitcast_fusion.1, bf16[2048,8,64]{0,2,1:T(8,128)(2,1)} %gather.32), kind=kLoop, calls=%fused_computation.29 | loop fusion | flops 2097152 | bytes 8390656 | tf_op jit(solution)/shard_map/jit(_where)/select_n | solution.py:142
  196.5 3.4 %fusion.54 = (f32[8,64]{1,0:T(8,128)S(1)}, f32[8,64,2066]{2,1,0:T(8,128)}) fusion(f32[2066]{0:T(1024)S(1)} %copy-done.18, bf16[18,8,64]{0,2,1:T(8,128)(2,1)S(1)} %bitcast.104, bf16[2048,8,64]{0,2,1:T(8,128)(2,1)S(1)} %get-tuple-element.28, bf16[64,8,32]{2,0,1:T(8,128)(2,1)S(1)} %copy-done.3, bf16[64,8,32]{2,0,1:T(8,128)(2,1)S(1)} %copy-done.5, ...), kind=kOutput, calls=%fused_computation.125 | convolution fusion | flops 143990272 | bytes 6554824 | tf_op jit(solution)/shard_map/rhd,nhd->hrn/dot_general | solution.py:162
  199.9 13.6 %pmax.7 = f32[8,64]{1,0:T(8,128)S(1)} all-reduce(f32[8,64]{1,0:T(8,128)S(1)} %get-tuple-element.49), channel_id=1, replica_groups=mesh['heads'=4,'seq'=8] {'seq'}, use_global_device_ids=true, to_apply=%region_12.13 | all-reduce | flops 512 | bytes 4096 | tf_op jit(solution)/shard_map/pmax | solution.py:172
  213.5 3.3 %fusion.2 = f32[8,64]{1,0:T(8,128)S(1)} fusion(f32[8,64,2066]{2,1,0:T(8,128)} %get-tuple-element.50, f32[8,64]{1,0:T(8,128)S(1)} %get-tuple-element.49, pred[64,2066]{1,0:T(8,128)(4,1)S(1)} %iota_compare_fusion), kind=kLoop, calls=%fused_computation.11 | loop fusion | flops 3172864 | bytes 4367488 | tf_op jit(solution)/shard_map/reduce_sum | solution.py:168
  216.8 13.6 %psum.38 = f32[8,64]{1,0:T(8,128)S(1)} all-reduce(f32[8,64]{1,0:T(8,128)S(1)} %get-tuple-element.6), channel_id=1, replica_groups=mesh['heads'=4,'seq'=8] {'seq'}, use_global_device_ids=true, to_apply=%region_15.16 | all-reduce | flops 512 | bytes 4096 | tf_op jit(solution)/shard_map/psum | solution.py:174
  230.4 4.6 %fusion.15 = f32[8,64,64]{2,1,0:T(8,128)} fusion(bf16[18,8,64]{0,2,1:T(8,128)(2,1)S(1)} %bitcast.103, bf16[2048,8,64]{0,2,1:T(8,128)(2,1)} %get-tuple-element.27, f32[8,64,2066]{2,1,0:T(8,128)} %get-tuple-element.50, f32[8,64]{1,0:T(8,128)S(1)} %get-tuple-element.49, pred[64,2066]{1,0:T(8,128)(4,1)S(1)} %iota_compare_fusion, f32[8,64]{1,0:T(8,128)S(1)} %get-tuple-element.7), kind=kOutput, calls=%fused_computation.31 | convolution fusion | flops 142834688 | bytes 6614144 | tf_op jit(solution)/shard_map/hrn,nhd->hrd/dot_general | solution.py:169
  235.0 53.2 %all-reduce.6.cloned.1.call-done = f32[8,64,64]{2,1,0:T(8,128)} async-done(((f32[8,64,64]{2,1,0:T(8,128)}), f32[8,64,64]{2,1,0:T(8,128)}) %all-reduce.6.cloned.1.call-update) | async-done | bytes 131088 | tf_op jit(solution)/shard_map/psum | solution.py:174
  288.2 1.3 fusion.26
  290.0 17.4 %psum.39 = bf16[64,256]{1,0:T(8,128)(2,1)} all-reduce(f32[64,256]{1,0:T(8,128)S(1)} %fusion.55), channel_id=1, replica_groups=mesh['heads'=4,'seq'=8] {'heads'}, use_global_device_ids=true, to_apply=%region_16.17 | all-reduce | flops 16384 | bytes 98304 | tf_op jit(solution)/shard_map/psum | solution.py:188
  (112 shorter events, 23.7 us)
Async XLA Ops:
  7.2 35.9 %copy-start = (bf16[18,128,512]{2,1,0:T(8,128)(2,1)S(1)}, bf16[18,128,512]{2,1,0:T(8,128)(2,1)}, u32[]{:S(2)}) copy-start(bf16[18,128,512]{2,1,0:T(8,128)(2,1)} %param.17) | copy-start | bytes 7077892
  7.2 147.1 %all-reduce.4.cloned.1.call-start = ((), (), s32[]{:S(2)}) async-start(), calls=%async_computation | async-start | bytes 1572864 | tf_op jit(solution)/shard_map/psum | solution.py:65
  13.5 44.7 %collective-permute-start.2 = (bf16[4,2]{0,1:T(2,128)(2,1)}, bf16[4,2]{0,1:T(2,128)(2,1)}, u32[]{:S(2)}, u32[]{:S(2)}) collective-permute-start(bf16[4,2]{0,1:T(2,128)(2,1)} %get-tuple-element.42), channel_id=1, source_target_pairs={{0,3},{1,4},{2,5},{3,6},{4,7},{5,0},{6,1},{7,2},{8,11},{9,12},{10,... | collective-permute-start | bytes 56 | tf_op jit(solution)/shard_map/ppermute | solution.py:23
  16.0 42.9 %collective-permute-start.1 = (bf16[4,2]{0,1:T(2,128)(2,1)}, bf16[4,2]{0,1:T(2,128)(2,1)}, u32[]{:S(2)}, u32[]{:S(2)}) collective-permute-start(bf16[4,2]{0,1:T(2,128)(2,1)} %get-tuple-element.43), channel_id=1, source_target_pairs={{0,2},{1,3},{2,4},{3,5},{4,6},{5,7},{6,0},{7,1},{8,10},{9,11},{10,... | collective-permute-start | bytes 56 | tf_op jit(solution)/shard_map/ppermute | solution.py:23
  17.6 44.3 %collective-permute-start = (bf16[4,2]{0,1:T(2,128)(2,1)}, bf16[4,2]{0,1:T(2,128)(2,1)}, u32[]{:S(2)}, u32[]{:S(2)}) collective-permute-start(bf16[4,2]{0,1:T(2,128)(2,1)} %get-tuple-element.44), channel_id=1, source_target_pairs={{0,1},{1,2},{2,3},{3,4},{4,5},{5,6},{6,7},{7,0},{8,9},{9,10},{10,1... | collective-permute-start | bytes 56 | tf_op jit(solution)/shard_map/ppermute | solution.py:23
  39.3 248.9 %all-reduce.6.cloned.1.call-start = ((), (), s32[]{:S(2)}) async-start(), calls=%async_computation.1 | async-start | bytes 524288 | tf_op jit(solution)/shard_map/psum | solution.py:174
  48.9 1.2 copy-start.11
  50.1 1.7 copy-start.1
  50.1 62.8 %collective-permute-start.8 = (bf16[4,128,512]{2,1,0:T(8,128)(2,1)}, bf16[4,128,512]{2,1,0:T(8,128)(2,1)}, u32[]{:S(2)}, u32[]{:S(2)}) collective-permute-start(bf16[4,128,512]{2,1,0:T(8,128)(2,1)} %get-tuple-element.9), channel_id=1, source_target_pairs={{0,3},{1,4},{2,5},{3,6},{4,7},{5,0},{6,1},{7,2},{8,11},{9,12},{10,... | collective-permute-start | bytes 1572872 | tf_op jit(solution)/shard_map/ppermute | solution.py:23
  50.2 107.2 %collective-permute-start.7 = (bf16[4,128,512]{2,1,0:T(8,128)(2,1)}, bf16[4,128,512]{2,1,0:T(8,128)(2,1)}, u32[]{:S(2)}, u32[]{:S(2)}) collective-permute-start(bf16[4,128,512]{2,1,0:T(8,128)(2,1)} %get-tuple-element.10), channel_id=1, source_target_pairs={{0,2},{1,3},{2,4},{3,5},{4,6},{5,7},{6,0},{7,1},{8,10},{9,11},{10,... | collective-permute-start | bytes 1572872 | tf_op jit(solution)/shard_map/ppermute | solution.py:23
  50.2 2.7 copy-start.17
  50.2 2.8 copy-start.16
  53.1 1.6 copy-start.9
  53.1 1.6 copy-start.10
  54.7 11.7 %copy-start.14 = (s32[18]{0:T(128)S(1)}, s32[18]{0:T(128)}, u32[]{:S(2)}) copy-start(s32[18]{0:T(128)} %get-tuple-element.33) | copy-start | bytes 220
  58.2 99.1 %collective-permute-start.6 = (bf16[4,128,512]{2,1,0:T(8,128)(2,1)}, bf16[4,128,512]{2,1,0:T(8,128)(2,1)}, u32[]{:S(2)}, u32[]{:S(2)}) collective-permute-start(bf16[4,128,512]{2,1,0:T(8,128)(2,1)} %get-tuple-element.11), channel_id=1, source_target_pairs={{0,1},{1,2},{2,3},{3,4},{4,5},{5,6},{6,7},{7,0},{8,9},{9,10},{10,1... | collective-permute-start | bytes 1572872 | tf_op jit(solution)/shard_map/ppermute | solution.py:23
  58.9 109.6 %collective-permute-start.5 = (bf16[4,128,512]{2,1,0:T(8,128)(2,1)}, bf16[4,128,512]{2,1,0:T(8,128)(2,1)}, u32[]{:S(2)}, u32[]{:S(2)}) collective-permute-start(bf16[4,128,512]{2,1,0:T(8,128)(2,1)} %get-tuple-element.13), channel_id=1, source_target_pairs={{0,3},{1,4},{2,5},{3,6},{4,7},{5,0},{6,1},{7,2},{8,11},{9,12},{10,... | collective-permute-start | bytes 1572872 | tf_op jit(solution)/shard_map/ppermute | solution.py:23
  61.9 106.6 %collective-permute-start.4 = (bf16[4,128,512]{2,1,0:T(8,128)(2,1)}, bf16[4,128,512]{2,1,0:T(8,128)(2,1)}, u32[]{:S(2)}, u32[]{:S(2)}) collective-permute-start(bf16[4,128,512]{2,1,0:T(8,128)(2,1)} %get-tuple-element.14), channel_id=1, source_target_pairs={{0,2},{1,3},{2,4},{3,5},{4,6},{5,7},{6,0},{7,1},{8,10},{9,11},{10,... | collective-permute-start | bytes 1572872 | tf_op jit(solution)/shard_map/ppermute | solution.py:23
  64.4 92.0 %copy-start.12 = (pred[16]{0:T(512)(128)(4,1)}, pred[16]{0:T(512)(128)(4,1)S(1)}, u32[]{:S(2)}) copy-start(pred[16]{0:T(512)(128)(4,1)S(1)} %fusion.37) | copy-start | bytes 52
  65.8 0.5 copy-start.15
  112.9 55.6 %collective-permute-start.3 = (bf16[4,128,512]{2,1,0:T(8,128)(2,1)}, bf16[4,128,512]{2,1,0:T(8,128)(2,1)}, u32[]{:S(2)}, u32[]{:S(2)}) collective-permute-start(bf16[4,128,512]{2,1,0:T(8,128)(2,1)} %get-tuple-element.15), channel_id=1, source_target_pairs={{0,1},{1,2},{2,3},{3,4},{4,5},{5,6},{6,7},{7,0},{8,9},{9,10},{10,1... | collective-permute-start | bytes 1572872 | tf_op jit(solution)/shard_map/ppermute | solution.py:23
  156.4 0.6 copy-start.2
  156.4 0.9 copy-start.4
  171.4 3.7 %copy-start.13 = (pred[16]{0:T(512)(128)(4,1)S(1)}, pred[16]{0:T(512)(128)(4,1)}, u32[]{:S(2)}) copy-start(pred[16]{0:T(512)(128)(4,1)} %copy-done.12) | copy-start | bytes 52
  192.6 3.9 %copy-start.3 = (bf16[64,8,32]{2,0,1:T(8,128)(2,1)S(1)}, bf16[64,8,32]{2,0,1:T(8,128)(2,1)}, u32[]{:S(2)}) copy-start(bf16[64,8,32]{2,0,1:T(8,128)(2,1)} %copy-done.2) | copy-start | bytes 98308
  192.6 3.9 %copy-start.5 = (bf16[64,8,32]{2,0,1:T(8,128)(2,1)S(1)}, bf16[64,8,32]{2,0,1:T(8,128)(2,1)}, u32[]{:S(2)}) copy-start(bf16[64,8,32]{2,0,1:T(8,128)(2,1)} %copy-done.4) | copy-start | bytes 98308
  192.6 3.9 %copy-start.8 = (bf16[18,512]{0,1:T(8,128)(2,1)S(1)}, bf16[18,512]{0,1:T(8,128)(2,1)}, u32[]{:S(2)}) copy-start(bf16[18,512]{0,1:T(8,128)(2,1)} %copy.49) | copy-start | bytes 55300
  192.6 3.9 %copy-start.18 = (f32[2066]{0:T(1024)S(1)}, f32[2066]{0:T(1024)}, u32[]{:S(2)}) copy-start(f32[2066]{0:T(1024)} %constant.81.clone.1) | copy-start | bytes 24796
  213.4 16.9 %copy-start.7 = (bf16[18,512]{0,1:T(8,128)(2,1)S(1)}, bf16[18,512]{0,1:T(8,128)(2,1)}, u32[]{:S(2)}) copy-start(bf16[18,512]{0,1:T(8,128)(2,1)} %copy.51) | copy-start | bytes 55300
  230.4 59.4 %copy-start.6 = (bf16[512,256]{1,0:T(8,128)(2,1)S(1)}, bf16[512,256]{1,0:T(8,128)(2,1)}, u32[]{:S(2)}) copy-start(bf16[512,256]{1,0:T(8,128)(2,1)} %param.12) | copy-start | bytes 786436
Sparse Core Ops, SparseCore 0:
  39.4 114.7 all-reduce.3
  235.1 53.0 all-reduce.5
where the time goes:
time: 315 us; the launch traced here: 314 us
  waiting for transfers between devices  140 us (44%)
  blocking collectives  60.3 us (19%)
  local copies, waits for them, and re-layouts  47.2 us (15%)
  other arithmetic  31.8 us (10%)
  between operations  14.4 us (5%)
  matrix products  11.3 us (4%)
  starting transfers between devices  9.6 us (3%)
    psum x1, waiting for transfers between devices, shards(): lax.psum((local_sum * factor, local_acc * factor[..., None]), 'seq')  53.2 us
    ppermute x9, waiting for transfers between devices, passed_along(): lax.ppermute(array, axis, [(i, (i + by) % count) for i in range(count)])  45.2 us
    psum x1, waiting for transfers between devices, shards(): lax.psum(partial_value, 'seq').reshape(requests, 3, heads_here, HDIM)  41.4 us
    psum x1, blocking collectives, shards(): attn_out = lax.psum(out_terms, 'heads').astype(jnp.bfloat16)  17.4 us
    psum x1, blocking collectives, shards(): total_sq = lax.psum(jnp.sum(widened * widened, axis=1), 'seq')  15.7 us
    psum x1, blocking collectives, shards(): lax.psum((local_sum * factor, local_acc * factor[..., None]), 'seq')  13.6 us
    pmax x1, blocking collectives, shards(): top_score = lax.pmax(local_top, 'seq')  13.6 us
    gather x3, local copies, waits for them, and re-layouts, shards(): recv_keys[picked]  12.4 us
  transfers between devices with their start and end apart: 11, of which 3 were waited for; matrix products, arithmetic and copies ran while one was open for 13% of the time, Pallas kernels for 0%

commit v1 on v0

v1 whole, which is shorter than its diff:
```python
import functools
import math

import jax
import jax.numpy as jnp
from jax import lax
from jax.experimental import pallas as pl
from jax.experimental.pallas import tpu as pltpu
from jax.sharding import PartitionSpec as P

D = 2048
HDIM = 64
ROWS = 128
HOPS = 4
CAP = 4
SLOT_DEV = 16

ROPE_BASE = 130000.0
NORM_EPSILON = 1e-05
MASKED_SCORE = -1e30
MESH = pl.DeviceIdType.MESH
F32 = jnp.float32
BF16 = jnp.bfloat16
HIGHEST = lax.Precision.HIGHEST


def pack_kernel(seq_count, keep, dest, req, keys, values, send_k, send_v, meta, count, sem):
    me = lax.axis_index("seq")
    n_blocks = keep.shape[0]
    for hop in range(HOPS):
        count[hop] = 0
        for place in range(CAP):
            meta[hop, 0, place] = -1
            meta[hop, 1, place] = -1
            meta[hop, 2, place] = 0

    def moves(g, hop, place):
        at = (hop - 1) * CAP + place
        return (
            pltpu.make_async_copy(keys.at[g], send_k.at[at], sem),
            pltpu.make_async_copy(values.at[g], send_v.at[at], sem),
        )

    def step(g, sent):
        kept = keep[g] == 1
        slot = dest[g]
        hop = lax.rem(slot // SLOT_DEV - me + seq_count, seq_count)
        hop = jnp.where(kept, hop, 0)
        place = count[hop]

        @pl.when(kept)
        def _():
            count[hop] = place + 1
            meta[hop, 0, place] = lax.rem(slot, SLOT_DEV)
            meta[hop, 1, place] = req[g]
            meta[hop, 2, place] = g

        away = kept & (hop > 0)

        @pl.when(away)
        def _():
            for move in moves(g, hop, place):
                move.start()

        return sent + away.astype(jnp.int32)

    sent = lax.fori_loop(0, n_blocks, step, jnp.int32(0))

    def drain(_, carry):
        for move in moves(0, 1, 0):
            move.wait()
        return carry

    lax.fori_loop(0, sent, drain, 0)


def place_kernel(meta, keys, values, recv_k, recv_v, out_k, out_v, out_req, zeros, sem):
    zeros[...] = jnp.zeros_like(zeros)
    for slot in range(SLOT_DEV):
        out_req[slot] = -1
    for hop in range(HOPS):
        for place in range(CAP):
            slot = meta[hop, 0, place]

            @pl.when(slot >= 0)
            def _():
                out_req[slot] = meta[hop, 1, place]
                if hop == 0:
                    g = meta[0, 2, place]
                    from_k, from_v = keys.at[g], values.at[g]
                else:
                    at = (hop - 1) * CAP + place
                    from_k, from_v = recv_k.at[at], recv_v.at[at]
                pltpu.make_async_copy(from_k, out_k.at[slot], sem).start()
                pltpu.make_async_copy(from_v, out_v.at[slot], sem).start()

    for slot in range(SLOT_DEV):

        @pl.when(out_req[slot] < 0)
        def _():
            pltpu.make_async_copy(zeros, out_k.at[slot], sem).start()
            pltpu.make_async_copy(zeros, out_v.at[slot], sem).start()

    for slot in range(SLOT_DEV):
        pltpu.make_async_copy(zeros, out_k.at[slot], sem).wait()
        pltpu.make_async_copy(zeros, out_v.at[slot], sem).wait()


def rows_of(ref, lead, each):
    if each % 8 == 0:
        return ref[...].reshape(lead * each, ref.shape[-1])
    return jnp.concatenate([ref[d] for d in range(lead)], axis=0)


def main_kernel(
    n,
    n_heads,
    hidden,
    w_qkv,
    w_out,
    cos,
    sin,
    onehot,
    onehot_t,
    first_t,
    same,
    keep,
    fold_w,
    meta,
    keys,
    values,
    send_k,
    send_v,
    recv_k,
    recv_v,
    recv_meta,
    out_fk,
    out_fv,
    out_attn,
    kbuf,
    vbuf,
    fk,
    fv,
    tops,
    sums,
    accs,
    sq_buf,
    part_send,
    part_recv,
    q_all,
    mix_send,
    mix_recv,
    mixed_all,
    head_buf,
    load_sem,
    bulk_sem,
    meta_sem,
    seq_sem,
    head_sem,
):
    me = lax.axis_index("seq")
    my_head = lax.axis_index("heads")
    requests = hidden.shape[0]
    each = requests // n
    n_blocks = kbuf.shape[0]
    width = kbuf.shape[2]
    heads_here = width // HDIM

    load_k = pltpu.make_async_copy(keys, kbuf, load_sem.at[0])
    load_v = pltpu.make_async_copy(values, vbuf, load_sem.at[1])
    load_k.start()
    load_v.start()

    barrier = pltpu.get_barrier_semaphore()

    def peers(body):
        if n <= 8:
            for k in range(1, n):
                body(k, lax.rem(me + k, n))
        else:

            def step(k, carry):
                body(k, lax.rem(me + k, n))
                return carry

            lax.fori_loop(1, n, step, 0)

    peers(
        lambda k, d: pl.semaphore_signal(barrier, inc=1, device_id={"seq": d}, device_id_type=MESH)
    )
    for k in range(1, n_heads):
        pl.semaphore_signal(
            barrier,
            inc=1,
            device_id={"heads": lax.rem(my_head + k, n_heads)},
            device_id_type=MESH,
        )

    wide = hidden[...].astype(F32)
    col = jnp.sum(wide * wide, axis=1, keepdims=True)
    eye = lax.broadcasted_iota(jnp.int32, (requests, 128), 0) == lax.broadcasted_iota(
        jnp.int32, (requests, 128), 1
    )
    row = jnp.sum(jnp.where(eye, col, 0.0), axis=0, keepdims=True)
    sq_buf[me] = jnp.broadcast_to(row, (8, 128))

    pl.semaphore_wait(barrier, n - 1 + n_heads - 1)

    def exchange(stage, source, target):
        def copy(k, d):
            return pltpu.make_async_remote_copy(
                src_ref=source(d),
                dst_ref=target.at[me],
                send_sem=seq_sem.at[2 * stage, k],
                recv_sem=seq_sem.at[2 * stage + 1, k],
                device_id={"seq": d},
                device_id_type=MESH,
            )

        return (
            lambda: peers(lambda k, d: copy(k, d).start()),
            lambda: peers(lambda k, d: copy(k, d).wait_recv()),
            lambda: peers(lambda k, d: copy(k, d).wait_send()),
        )

    bulk = []
    for hop in range(1, HOPS):
        for which, (source, target) in enumerate(((send_k, recv_k), (send_v, recv_v))):
            at = pl.ds((hop - 1) * CAP, CAP)
            bulk.append(
                pltpu.make_async_remote_copy(
                    src_ref=source.at[at],
                    dst_ref=target.at[at],
                    send_sem=bulk_sem.at[0, 2 * hop - 2 + which],
                    recv_sem=bulk_sem.at[1, 2 * hop - 2 + which],
                    device_id={"seq": lax.rem(me + hop, n)},
                    device_id_type=MESH,
                )
            )
    metas = [
        pltpu.make_async_remote_copy(
            src_ref=meta.at[hop],
            dst_ref=recv_meta.at[hop],
            send_sem=meta_sem.at[0, hop],
            recv_sem=meta_sem.at[1, hop],
            device_id={"seq": lax.rem(me + hop, n)},
            device_id_type=MESH,
        )
        for hop in range(1, HOPS)
    ]

    sq_start, sq_wait, sq_done = exchange(0, lambda d: sq_buf.at[me], sq_buf)
    sq_start()
    for copy in metas:
        copy.start()
    for copy in bulk:
        copy.start()
    recv_meta[0] = meta[0]

    load_k.wait()
    load_v.wait()
    line = lax.broadcasted_iota(jnp.int32, (8, ROWS), 0)

    def fold(g, carry):
        weights = fold_w[pl.ds(g, 1), :]
        high = weights.astype(BF16).astype(F32)
        rest = weights - high
        middle = rest.astype(BF16).astype(F32)
        low = rest - middle
        stacked = jnp.where(
            line == 0, high, jnp.where(line == 1, middle, jnp.where(line == 2, low, 0.0))
        ).astype(BF16)
        total = jnp.sum(weights, axis=1, keepdims=True)
        folded_k = jnp.dot(stacked, kbuf[g], preferred_element_type=F32)
        folded_v = jnp.dot(stacked, vbuf[g], preferred_element_type=F32)
        fk[pl.ds(g, 1), :] = (
            (jnp.sum(folded_k, axis=0, keepdims=True) / total).astype(BF16).astype(F32)
        )
        fv[pl.ds(g, 1), :] = (
            (jnp.sum(folded_v, axis=0, keepdims=True) / total).astype(BF16).astype(F32)
        )
        return carry

    lax.fori_loop(0, n_blocks, fold, 0)
    out_fk[...] = jnp.where(keep[...] > 0.5, 0.0, fk[...]).astype(BF16)
    out_fv[...] = jnp.where(keep[...] > 0.5, 0.0, fv[...]).astype(BF16)

    sq_wait()
    row = jnp.sum(sq_buf[...], axis=0)[0:1, :]
    col = jnp.sum(jnp.where(eye, row, 0.0), axis=1, keepdims=True)
    normed = (wide * lax.rsqrt(col / D + NORM_EPSILON)).astype(BF16)
    for part in range(3):
        product = jnp.dot(normed, w_qkv[part], preferred_element_type=F32)
        for d in range(n):
            part_send[d, part] = product[d * each : (d + 1) * each]
    part_start, part_wait, part_done = exchange(1, lambda d: part_send.at[d], part_recv)
    part_start()
    part_recv[me] = part_send[me]
    part_wait()
    proj = [jnp.sum(part_recv[:, part], axis=0) for part in range(3)]

    lane = lax.broadcasted_iota(jnp.int32, (each, width), 1)
    lower = lax.rem(lane, HDIM) < HDIM // 2
    my_cos, my_sin = cos[me], sin[me]

    def rotated(x):
        ahead = jnp.concatenate([x[:, HDIM // 2 :], x[:, : HDIM // 2]], axis=1)
        behind = jnp.concatenate([x[:, -(HDIM // 2) :], x[:, : -(HDIM // 2)]], axis=1)
        return (x * my_cos + jnp.where(lower, ahead, behind) * my_sin).astype(BF16).astype(F32)

    query = rotated(proj[0])
    new_key = rotated(proj[1])
    new_value = proj[2].astype(BF16).astype(F32)
    q_all[me] = query
    q_start, q_wait, q_done = exchange(2, lambda d: q_all.at[me], q_all)
    q_start()
    q_wait()

    q_rows = rows_of(q_all, n, each).astype(BF16)
    accs[...] = jnp.dot(onehot[...].astype(BF16), q_rows, preferred_element_type=F32)
    head_mask = (
        lax.broadcasted_iota(jnp.int32, (heads_here, width), 1) // HDIM
        == lax.broadcasted_iota(jnp.int32, (heads_here, width), 0)
    )

    def spread(column):
        return jnp.sum(jnp.where(head_mask, column, 0.0), axis=0, keepdims=True)

    def attend(g, carry):
        query_g = jnp.where(head_mask, accs[pl.ds(g, 1), :], 0.0)
        scores = (
            lax.dot_general(
                query_g.astype(BF16),
                kbuf[g],
                (((1,), (1,)), ((), ())),
                preferred_element_type=F32,
            )
            * 0.125
        )
        top = jnp.max(scores, axis=1, keepdims=True)
        expo = jnp.exp(scores - top)
        total = jnp.sum(expo, axis=1, keepdims=True)
        mix = jnp.dot(expo.astype(BF16), vbuf[g], preferred_element_type=F32)
        mix = jnp.sum(jnp.where(head_mask, mix, 0.0), axis=0, keepdims=True)
        folded_score = jnp.sum(
            query_g * fk[pl.ds(g, 1), :], axis=1, keepdims=True
        ) * 0.125 + math.log(ROWS)
        kept = keep[pl.ds(g, 1), :] > 0.5
        tops[pl.ds(g, 1), :] = jnp.where(kept, spread(top), spread(folded_score))
        sums[pl.ds(g, 1), :] = jnp.where(kept, spread(total), 1.0)
        accs[pl.ds(g, 1), :] = jnp.where(kept, mix, fv[pl.ds(g, 1), :])
        return carry

    lax.fori_loop(0, n_blocks, attend, 0)
    block_tops = tops[...]
    req_top = jnp.full_like(block_tops, MASKED_SCORE)
    for g in range(n_blocks):
        req_top = jnp.maximum(
            req_top, jnp.where(same[:, g : g + 1] > 0.5, block_tops[g : g + 1], MASKED_SCORE)
        )
    factor = jnp.exp(block_tops - req_top)

    def by_request(table, array):
        return jnp.dot(table[...], array, precision=HIGHEST, preferred_element_type=F32)

    present = jnp.sum(first_t[...], axis=1, keepdims=True)
    top_rows = jnp.where(present > 0.5, by_request(first_t, req_top), MASKED_SCORE)
    sum_rows = by_request(onehot_t, sums[...] * factor)
    acc_rows = by_request(onehot_t, accs[...] * factor)
    for part, rows in enumerate((top_rows, sum_rows, acc_rows)):
        for d in range(n):
            mix_send[d, part] = rows[d * each : (d + 1) * each]
    mix_start, mix_wait, mix_done = exchange(3, lambda d: mix_send.at[d], mix_recv)
    mix_start()
    mix_recv[me] = mix_send[me]

    block_diag = (
        lax.broadcasted_iota(jnp.int32, (width, width), 0) // HDIM
        == lax.broadcasted_iota(jnp.int32, (width, width), 1) // HDIM
    ).astype(F32)
    own_score = (
        jnp.dot(query * new_key, block_diag, precision=HIGHEST, preferred_element_type=F32) * 0.125
    )
    mix_wait()
    all_tops = mix_recv[:, 0]
    final_top = jnp.maximum(jnp.max(all_tops, axis=0), own_score)
    scale = jnp.exp(all_tops - final_top[None])
    own_expo = jnp.exp(own_score - final_top)
    totals = jnp.sum(mix_recv[:, 1] * scale, axis=0) + own_expo
    mixture = (
        jnp.sum(mix_recv[:, 2] * scale, axis=0) + own_expo.astype(BF16).astype(F32) * new_value
    )
    mixed_all[me] = (mixture / totals).astype(BF16).astype(F32)
    mixed_start, mixed_wait, mixed_done = exchange(4, lambda d: mixed_all.at[me], mixed_all)
    mixed_start()
    mixed_wait()

    mixed_rows = rows_of(mixed_all, n, each).astype(BF16)
    head_buf[my_head] = jnp.dot(mixed_rows, w_out[...], preferred_element_type=F32)
    head_copies = [
        pltpu.make_async_remote_copy(
            src_ref=head_buf.at[my_head],
            dst_ref=head_buf.at[my_head],
            send_sem=head_sem.at[0, k],
            recv_sem=head_sem.at[1, k],
            device_id={"heads": lax.rem(my_head + k, n_heads)},
            device_id_type=MESH,
        )
        for k in range(1, n_heads)
    ]
    for copy in head_copies:
        copy.start()
    for copy in head_copies:
        copy.wait_recv()
    total = head_buf[0]
    for h in range(1, n_heads):
        total = total + head_buf[h]
    out_attn[...] = total.astype(BF16)

    for done in (sq_done, part_done, q_done, mix_done, mixed_done):
        done()
    for copy in head_copies:
        copy.wait_send()
    for copy in metas + bulk:
        copy.wait()


def shards(
    n,
    n_heads,
    hidden,
    w_qkv,
    w_out,
    positions,
    req_blocks,
    keep_list,
    dest_slot,
    key_cache,
    value_cache,
    fold_weight,
):
    requests = hidden.shape[0]
    n_blocks, row_count, width = key_cache.shape
    me = lax.axis_index("seq")
    each = requests // n
    moved = (HOPS - 1) * CAP

    ids = jnp.arange(requests, dtype=jnp.int32)
    ends = jnp.sum(jnp.where(ids[None, :] <= ids[:, None], req_blocks[None, :], 0), axis=1)
    block_ids = jnp.arange(n_blocks, dtype=jnp.int32)
    global_ids = me * n_blocks + block_ids
    blk_req = jnp.sum((global_ids[:, None] >= ends[None, :]).astype(jnp.int32), axis=1)
    onehot = (blk_req[:, None] == ids[None, :]).astype(F32)
    onehot_t = (blk_req[None, :] == ids[:, None]).astype(F32)
    same_bool = blk_req[:, None] == blk_req[None, :]
    same = same_bool.astype(F32)
    has_earlier = jnp.any(same_bool & (block_ids[None, :] < block_ids[:, None]), axis=1)
    first_t = jnp.where(has_earlier[None, :], 0.0, onehot_t)
    keep_rows = jnp.broadcast_to((keep_list == 1).astype(F32)[:, None], (n_blocks, width))

    half = HDIM // 2
    freqs = ROPE_BASE ** (-(2.0 * jnp.arange(half, dtype=F32)) / HDIM)
    angles = positions.astype(F32)[:, None] * freqs[None, :]
    cos_half, sin_half = jnp.cos(angles), jnp.sin(angles)
    copies = width // HDIM
    cos = jnp.tile(jnp.concatenate([cos_half, cos_half], axis=1), (1, copies))
    sin = jnp.tile(jnp.concatenate([-sin_half, sin_half], axis=1), (1, copies))
    cos = cos.reshape(n, each, width)
    sin = sin.reshape(n, each, width)

    smem = pl.BlockSpec(memory_space=pltpu.SMEM)
    vmem = pl.BlockSpec(memory_space=pltpu.VMEM)
    hbm = pl.BlockSpec(memory_space=pl.ANY)
    moved_shape = jax.ShapeDtypeStruct((moved, row_count, width), BF16)
    meta_shape = jax.ShapeDtypeStruct((HOPS, 8, 128), jnp.int32)
    folded_shape = jax.ShapeDtypeStruct((n_blocks, width), BF16)

    send_k, send_v, meta = pl.pallas_call(
        functools.partial(pack_kernel, n),
        out_shape=(moved_shape, moved_shape, meta_shape),
        in_specs=[smem, smem, smem, hbm, hbm],
        out_specs=(hbm, hbm, smem),
        scratch_shapes=[pltpu.SMEM((HOPS,), jnp.int32), pltpu.SemaphoreType.DMA],
        name="pack_blocks",
    )(keep_list, dest_slot, blk_req, key_cache, value_cache)

    block_rows = pltpu.VMEM((n_blocks, width), F32)
    request_rows = pltpu.VMEM((n, each, width), F32)
    three_parts = pltpu.VMEM((n, 3, each, width), F32)
    recv_k, recv_v, recv_meta, folded_keys, folded_values, attn_out = pl.pallas_call(
        functools.partial(main_kernel, n, n_heads),
        out_shape=(
            moved_shape,
            moved_shape,
            meta_shape,
            folded_shape,
            folded_shape,
            jax.ShapeDtypeStruct((requests, w_out.shape[1]), BF16),
        ),
        in_specs=[vmem] * 12 + [hbm] * 4,
        out_specs=(hbm, hbm, vmem, vmem, vmem, vmem),
        scratch_shapes=[
            pltpu.VMEM((n_blocks, row_count, width), BF16),
            pltpu.VMEM((n_blocks, row_count, width), BF16),
            block_rows,
            block_rows,
            block_rows,
            block_rows,
            block_rows,
            pltpu.VMEM((n, 8, 128), F32),
            three_parts,
            three_parts,
            request_rows,
            three_parts,
            three_parts,
            request_rows,
            pltpu.VMEM((n_heads, requests, w_out.shape[1]), F32),
            pltpu.SemaphoreType.DMA((2,)),
            pltpu.SemaphoreType.DMA((2, 2 * (HOPS - 1))),
            pltpu.SemaphoreType.DMA((2, HOPS)),
            pltpu.SemaphoreType.DMA((10, n)),
            pltpu.SemaphoreType.DMA((2, n_heads)),
        ],
        compiler_params=pltpu.CompilerParams(
            collective_id=0, has_side_effects=True, vmem_limit_bytes=48 * 2**20
        ),
        name="decode_and_move",
    )(
        hidden,
        jnp.transpose(w_qkv, (1, 0, 2)),
        w_out,
        cos,
        sin,
        onehot,
        onehot_t,
        first_t,
        same,
        keep_rows,
        fold_weight,
        meta,
        key_cache,
        value_cache,
        send_k,
        send_v,
    )

    packed_shape = jax.ShapeDtypeStruct((SLOT_DEV, row_count, width), BF16)
    packed_keys, packed_values, packed_request = pl.pallas_call(
        place_kernel,
        out_shape=(packed_shape, packed_shape, jax.ShapeDtypeStruct((SLOT_DEV,), jnp.int32)),
        in_specs=[smem, hbm, hbm, hbm, hbm],
        out_specs=(hbm, hbm, smem),
        scratch_shapes=[pltpu.VMEM((row_count, width), BF16), pltpu.SemaphoreType.DMA],
        name="place_blocks",
    )(recv_meta, key_cache, value_cache, recv_k, recv_v)
    return (packed_keys, packed_values, packed_request, folded_keys, folded_values, attn_out)


def solution(mesh):
    return jax.shard_map(
        functools.partial(shards, mesh.shape["seq"], mesh.shape["heads"]),
        mesh=mesh,
        in_specs=(
            P(None, "seq"),
            P("seq", None, "heads"),
            P("heads", "seq"),
            P(),
            P(),
            P("seq"),
            P("seq"),
            P("seq", None, "heads"),
            P("seq", None, "heads"),
            P("seq", None),
        ),
        out_specs=(
            P("seq", None, "heads"),
            P("seq", None, "heads"),
            P("seq"),
            P("seq", "heads"),
            P("seq", "heads"),
            P(None, "seq"),
        ),
        check_vma=False,
    )
```

time: 315 us -> 343 us (1.089)
  the two profiles are of different devices: /device:TPU:0 before, /device:TPU:1 now
where the time goes in v1:
time: 343 us
  Pallas kernels  334 us (97%)
  local copies, waits for them, and re-layouts  5.83 us (2%)
    pallas_call x1, Pallas kernels, shards(): pl.pallas_call(functools.partial(main_kernel, n, n_heads), out_shape=(mov...  130 us
    pallas_call x1, Pallas kernels, shards(): pl.pallas_call(place_kernel, out_shape=(packed_shape, packed_shape, jax.S...  130 us
    pallas_call x1, Pallas kernels, shards(): pl.pallas_call(functools.partial(pack_kernel, n), out_shape=(moved_shape,...  74.3 us

profile of v1, /device:TPU:1, one launch (start us, length us, event | category | flops | bytes accessed | tf_op | source)
XLA Modules:
  0.0 343.2 jit_solution(13531921649167665331)
XLA Ops:
  0.6 0.7 convert_element_type.18
  1.3 0.8 select_reduce_fusion
  2.1 0.2 convert_reduce_fusion.req
  2.3 0.0 copy-start.8
  2.3 0.7 compare_convert_fusion.1
  2.9 0.1 fusion.1.onehot
  3.0 0.2 compare_convert_fusion
  3.2 0.1 broadcast_in_dim.30.keep
  3.3 0.2 fusion.3
  3.5 0.1 pad_maximum_fusion
  3.6 0.1 tile.17.cos
  3.8 0.1 tile.19.sin
  3.9 0.0 copy-done.8
  3.9 0.0 copy-start.2
  3.9 0.0 copy-start.3
  3.9 0.0 copy-start.4
  3.9 0.0 copy-start.7
  3.9 74.3 %pack_blocks.1 = (bf16[12,128,512]{2,1,0:T(8,128)(2,1)}, bf16[12,128,512]{2,1,0:T(8,128)(2,1)}, s32[4,8,128]{2,1,0:T(8,128)}) custom-call(s32[18]{0:T(128)} %keep.1, s32[18]{0:T(128)} %dest.1, s32[18]{0:T(128)} %copy-done.8, bf16[18,128,512]{2,1,0:T(8,128)(2,1)} %keys.5, bf16[18,128,512]{2,1,0:T(8,128)(2,1)} %values.5), custom_call_target="tpu_custom_call" | custom-call | tf_op jit(solution)/shard_map/pack_blocks/pallas_call | solution.py:478
  78.2 0.0 copy-done.2
  78.3 0.0 copy-done.3
  78.3 0.0 copy-done.4
  78.3 0.0 copy-done.7
  78.3 0.0 copy-start.6
  78.3 0.7 copy-done.6
  79.0 129.9 %decode_and_move.1 = (bf16[12,128,512]{2,1,0:T(8,128)(2,1)S(1)}, bf16[12,128,512]{2,1,0:T(8,128)(2,1)S(1)}, s32[4,8,128]{2,1,0:T(8,128)S(1)}, bf16[18,512]{1,0:T...) custom-call(bf16[64,256]{1,0:T(8,128)(2,1)S(1)} %copy-done.4, ...), custom_call_target="tpu_custom_call" | custom-call | tf_op jit(solution)/shard_map/decode_and_move/pallas_call | solution.py:490
  208.9 1.1 copy-done
  210.0 1.2 copy-done.1
  211.2 0.6 copy-done.5
  211.8 129.6 %place_blocks.1 = (bf16[16,128,512]{2,1,0:T(8,128)(2,1)}, bf16[16,128,512]{2,1,0:T(8,128)(2,1)}, s32[16]{0:T(128)}) custom-call(s32[4,8,128]{2,1,0:T(8,128)} %copy-done.5, bf16[18,128,512]{2,1,0:T(8,128)(2,1)} %keys.5, bf16[18,128,512]{2,1,0:T(8,128)(2,1)} %values.5, bf16[12,128,512]{2,1,0:T(8,128)(2,1)} %copy-done, bf16[12,128,512]{2,1,0:T(8,128)(2,1)} %copy-done.1), custom_call_target="tpu_custom_call" | custom-call | tf_op jit(solution)/shard_map/place_blocks/pallas_call | solution.py:548
  341.4 0.6 copy.19
  342.0 0.6 copy.20
  342.6 0.6 copy.21
  (9 shorter events, 0.1 us)
Async XLA Ops:
  2.3 1.6 copy-start.8
  3.9 74.4 %copy-start.2 = (bf16[256,3,512]{2,0,1:T(8,128)(2,1)S(1)}, bf16[256,3,512]{2,0,1:T(8,128)(2,1)}, u32[]{:S(2)}) copy-start(bf16[256,3,512]{2,0,1:T(8,128)(2,1)} %param.11) | copy-start | bytes 2359300
  3.9 74.4 %copy-start.3 = (bf16[512,256]{1,0:T(8,128)(2,1)S(1)}, bf16[512,256]{1,0:T(8,128)(2,1)}, u32[]{:S(2)}) copy-start(bf16[512,256]{1,0:T(8,128)(2,1)} %w_out.1) | copy-start | bytes 786436
  3.9 74.4 %copy-start.4 = (bf16[64,256]{1,0:T(8,128)(2,1)S(1)}, bf16[64,256]{1,0:T(8,128)(2,1)}, u32[]{:S(2)}) copy-start(bf16[64,256]{1,0:T(8,128)(2,1)} %hidden.1) | copy-start | bytes 98308
  3.9 74.4 %copy-start.7 = (f32[18,128]{1,0:T(8,128)S(1)}, f32[18,128]{1,0:T(8,128)}, u32[]{:S(2)}) copy-start(f32[18,128]{1,0:T(8,128)} %fold_w.1) | copy-start | bytes 27652
  78.3 0.7 copy-start.6
  208.9 1.2 copy-start
  210.0 1.2 copy-start.1
  211.2 0.6 copy-start.5

commit v2 on v1

--- a/solution.py
+++ b/solution.py
@@ -14,6 +14,8 @@
 HOPS = 4
 CAP = 4
 SLOT_DEV = 16
+TURNS = (6, 3, 0, 3, 0, 12)
+GROUP = 6
 
 ROPE_BASE = 130000.0
 NORM_EPSILON = 1e-05
@@ -24,7 +26,7 @@
 HIGHEST = lax.Precision.HIGHEST
 
 
-def pack_kernel(seq_count, keep, dest, req, keys, values, send_k, send_v, meta, count, sem):
+def pack_kernel(seq_count, keep, dest, req, keys, values, own_k, own_v, send_k, send_v, meta, count):
     me = lax.axis_index("seq")
     n_blocks = keep.shape[0]
     for hop in range(HOPS):
@@ -32,65 +34,49 @@
         for place in range(CAP):
             meta[hop, 0, place] = -1
             meta[hop, 1, place] = -1
-            meta[hop, 2, place] = 0
-
-    def moves(g, hop, place):
-        at = (hop - 1) * CAP + place
-        return (
-            pltpu.make_async_copy(keys.at[g], send_k.at[at], sem),
-            pltpu.make_async_copy(values.at[g], send_v.at[at], sem),
-        )
-
-    def step(g, sent):
-        kept = keep[g] == 1
+
+    def step(g, carry):
         slot = dest[g]
         hop = lax.rem(slot // SLOT_DEV - me + seq_count, seq_count)
-        hop = jnp.where(kept, hop, 0)
-        place = count[hop]
+        kept = keep[g] == 1
 
         @pl.when(kept)
         def _():
+            place = count[hop]
             count[hop] = place + 1
             meta[hop, 0, place] = lax.rem(slot, SLOT_DEV)
             meta[hop, 1, place] = req[g]
-            meta[hop, 2, place] = g
-
-        away = kept & (hop > 0)
-
-        @pl.when(away)
-        def _():
-            for move in moves(g, hop, place):
-                move.start()
-
-        return sent + away.astype(jnp.int32)
-
-    sent = lax.fori_loop(0, n_blocks, step, jnp.int32(0))
-
-    def drain(_, carry):
-        for move in moves(0, 1, 0):
-            move.wait()
+
+            @pl.when(hop == 0)
+            def _():
+                own_k[place] = keys[g]
+                own_v[place] = values[g]
+
+            @pl.when(hop > 0)
+            def _():
+                at = (hop - 1) * CAP + place
+                send_k[at] = keys[g]
+                send_v[at] = values[g]
+
         return carry
 
-    lax.fori_loop(0, sent, drain, 0)
-
-
-def place_kernel(meta, keys, values, recv_k, recv_v, out_k, out_v, out_req, zeros, sem):
+    lax.fori_loop(0, n_blocks, step, 0)
+
+
+def place_kernel(meta, own_k, own_v, recv_k, recv_v, out_k, out_v, out_req, zeros, sem):
     zeros[...] = jnp.zeros_like(zeros)
     for slot in range(SLOT_DEV):
         out_req[slot] = -1
     for hop in range(HOPS):
         for place in range(CAP):
             slot = meta[hop, 0, place]
+            at = (hop - 1) * CAP + place
+            from_k = own_k.at[place] if hop == 0 else recv_k.at[at]
+            from_v = own_v.at[place] if hop == 0 else recv_v.at[at]
 
             @pl.when(slot >= 0)
             def _():
                 out_req[slot] = meta[hop, 1, place]
-                if hop == 0:
-                    g = meta[0, 2, place]
-                    from_k, from_v = keys.at[g], values.at[g]
-                else:
-                    at = (hop - 1) * CAP + place
-                    from_k, from_v = recv_k.at[at], recv_v.at[at]
                 pltpu.make_async_copy(from_k, out_k.at[slot], sem).start()
                 pltpu.make_async_copy(from_v, out_v.at[slot], sem).start()
 
@@ -223,20 +209,27 @@
             lambda: peers(lambda k, d: copy(k, d).wait_send()),
         )
 
-    bulk = []
-    for hop in range(1, HOPS):
-        for which, (source, target) in enumerate(((send_k, recv_k), (send_v, recv_v))):
-            at = pl.ds((hop - 1) * CAP, CAP)
-            bulk.append(
-                pltpu.make_async_remote_copy(
-                    src_ref=source.at[at],
-                    dst_ref=target.at[at],
-                    send_sem=bulk_sem.at[0, 2 * hop - 2 + which],
-                    recv_sem=bulk_sem.at[1, 2 * hop - 2 + which],
-                    device_id={"seq": lax.rem(me + hop, n)},
-                    device_id_type=MESH,
-                )
+    def block_copies(pair):
+        hop, place = HOPS - 1 - pair // CAP, pair % CAP
+        at = (hop - 1) * CAP + place
+        return [
+            pltpu.make_async_remote_copy(
+                src_ref=source.at[at],
+                dst_ref=target.at[at],
+                send_sem=bulk_sem.at[which, at],
+                recv_sem=bulk_sem.at[which + 2, at],
+                device_id={"seq": lax.rem(me + hop, n)},
+                device_id_type=MESH,
             )
+            for which, (source, target) in enumerate(((send_k, recv_k), (send_v, recv_v)))
+        ]
+
+    bulk = [copy for pair in range((HOPS - 1) * CAP) for copy in block_copies(pair)]
+
+    def send_blocks(turn):
+        for copy in bulk[sum(TURNS[:turn]) : sum(TURNS[: turn + 1])]:
+            copy.start()
+
     metas = [
         pltpu.make_async_remote_copy(
             src_ref=meta.at[hop],
@@ -253,15 +246,24 @@
     sq_start()
     for copy in metas:
         copy.start()
-    for copy in bulk:
-        copy.start()
+    send_blocks(0)
     recv_meta[0] = meta[0]
 
     load_k.wait()
     load_v.wait()
     line = lax.broadcasted_iota(jnp.int32, (8, ROWS), 0)
 
-    def fold(g, carry):
+    def in_groups(body):
+        group = GROUP if n_blocks % GROUP == 0 else 1
+
+        def some(i, carry):
+            for j in range(group):
+                body(i * group + j)
+            return carry
+
+        lax.fori_loop(0, n_blocks // group, some, 0)
+
+    def fold(g):
         weights = fold_w[pl.ds(g, 1), :]
         high = weights.astype(BF16).astype(F32)
         rest = weights - high
@@ -279,9 +281,8 @@
         fv[pl.ds(g, 1), :] = (
             (jnp.sum(folded_v, axis=0, keepdims=True) / total).astype(BF16).astype(F32)
         )
-        return carry
-
-    lax.fori_loop(0, n_blocks, fold, 0)
+
+    in_groups(fold)
     out_fk[...] = jnp.where(keep[...] > 0.5, 0.0, fk[...]).astype(BF16)
     out_fv[...] = jnp.where(keep[...] > 0.5, 0.0, fv[...]).astype(BF16)
 
@@ -295,6 +296,7 @@
             part_send[d, part] = product[d * each : (d + 1) * each]
     part_start, part_wait, part_done = exchange(1, lambda d: part_send.at[d], part_recv)
     part_start()
+    send_blocks(1)
     part_recv[me] = part_send[me]
     part_wait()
     proj = [jnp.sum(part_recv[:, part], axis=0) for part in range(3)]
@@ -314,6 +316,7 @@
     q_all[me] = query
     q_start, q_wait, q_done = exchange(2, lambda d: q_all.at[me], q_all)
     q_start()
+    send_blocks(2)
     q_wait()
 
     q_rows = rows_of(q_all, n, each).astype(BF16)
@@ -326,7 +329,7 @@
     def spread(column):
         return jnp.sum(jnp.where(head_mask, column, 0.0), axis=0, keepdims=True)
 
-    def attend(g, carry):
+    def attend(g):
         query_g = jnp.where(head_mask, accs[pl.ds(g, 1), :], 0.0)
         scores = (
             lax.dot_general(
@@ -349,9 +352,8 @@
         tops[pl.ds(g, 1), :] = jnp.where(kept, spread(top), spread(folded_score))
         sums[pl.ds(g, 1), :] = jnp.where(kept, spread(total), 1.0)
         accs[pl.ds(g, 1), :] = jnp.where(kept, mix, fv[pl.ds(g, 1), :])
-        return carry
-
-    lax.fori_loop(0, n_blocks, attend, 0)
+
+    in_groups(attend)
     block_tops = tops[...]
     req_top = jnp.full_like(block_tops, MASKED_SCORE)
     for g in range(n_blocks):
@@ -363,36 +365,52 @@
     def by_request(table, array):
         return jnp.dot(table[...], array, precision=HIGHEST, preferred_element_type=F32)
 
+    stat_lane = lax.broadcasted_iota(jnp.int32, (width, 128), 1)
+    stat_row = lax.broadcasted_iota(jnp.int32, (width, 128), 0)
+    pick_head = (stat_row == stat_lane * HDIM).astype(F32)
+    sum_head = (stat_row // HDIM == stat_lane).astype(F32)
+
+    def exact(left, right):
+        return jnp.dot(left, right, precision=HIGHEST, preferred_element_type=F32)
+
     present = jnp.sum(first_t[...], axis=1, keepdims=True)
-    top_rows = jnp.where(present > 0.5, by_request(first_t, req_top), MASKED_SCORE)
-    sum_rows = by_request(onehot_t, sums[...] * factor)
+    top_rows = by_request(first_t, exact(req_top, pick_head))
+    top_rows = jnp.where(present > 0.5, top_rows, MASKED_SCORE)
+    sum_rows = by_request(onehot_t, exact(sums[...] * factor, pick_head))
     acc_rows = by_request(onehot_t, accs[...] * factor)
-    for part, rows in enumerate((top_rows, sum_rows, acc_rows)):
-        for d in range(n):
-            mix_send[d, part] = rows[d * each : (d + 1) * each]
+    for d in range(n):
+        own_rows = slice(d * each, (d + 1) * each)
+        mix_send[d, :, :width] = acc_rows[own_rows]
+        mix_send[d, :, width : width + 128] = top_rows[own_rows]
+        mix_send[d, :, width + 128 :] = sum_rows[own_rows]
     mix_start, mix_wait, mix_done = exchange(3, lambda d: mix_send.at[d], mix_recv)
     mix_start()
+    send_blocks(3)
     mix_recv[me] = mix_send[me]
 
-    block_diag = (
-        lax.broadcasted_iota(jnp.int32, (width, width), 0) // HDIM
-        == lax.broadcasted_iota(jnp.int32, (width, width), 1) // HDIM
+    spread_head = (
+        lax.broadcasted_iota(jnp.int32, (128, width), 1) // HDIM
+        == lax.broadcasted_iota(jnp.int32, (128, width), 0)
     ).astype(F32)
-    own_score = (
-        jnp.dot(query * new_key, block_diag, precision=HIGHEST, preferred_element_type=F32) * 0.125
-    )
+    own_score = exact(query * new_key, sum_head) * 0.125
     mix_wait()
-    all_tops = mix_recv[:, 0]
+    all_tops = mix_recv[:, :, width : width + 128]
     final_top = jnp.maximum(jnp.max(all_tops, axis=0), own_score)
     scale = jnp.exp(all_tops - final_top[None])
     own_expo = jnp.exp(own_score - final_top)
-    totals = jnp.sum(mix_recv[:, 1] * scale, axis=0) + own_expo
-    mixture = (
-        jnp.sum(mix_recv[:, 2] * scale, axis=0) + own_expo.astype(BF16).astype(F32) * new_value
-    )
-    mixed_all[me] = (mixture / totals).astype(BF16).astype(F32)
+    totals = jnp.sum(mix_recv[:, :, width + 128 :] * scale, axis=0) + own_expo
+    own_prob = own_expo.astype(BF16).astype(F32)
+    mixture = exact(own_prob, spread_head) * new_value
+    if each % 8 == 0:
+        wide_scale = exact(scale.reshape(n * each, 128), spread_head).reshape(n, each, width)
+        mixture = mixture + jnp.sum(mix_recv[:, :, :width] * wide_scale, axis=0)
+    else:
+        for d in range(n):
+            mixture = mixture + mix_recv[d, :, :width] * exact(scale[d], spread_head)
+    mixed_all[me] = (mixture / exact(totals, spread_head)).astype(BF16).astype(F32)
     mixed_start, mixed_wait, mixed_done = exchange(4, lambda d: mixed_all.at[me], mixed_all)
     mixed_start()
+    send_blocks(4)
     mixed_wait()
 
     mixed_rows = rows_of(mixed_all, n, each).astype(BF16)
@@ -410,6 +428,7 @@
     ]
     for copy in head_copies:
         copy.start()
+    send_blocks(5)
     for copy in head_copies:
         copy.wait_recv()
     total = head_buf[0]
@@ -472,20 +491,23 @@
     vmem = pl.BlockSpec(memory_space=pltpu.VMEM)
     hbm = pl.BlockSpec(memory_space=pl.ANY)
     moved_shape = jax.ShapeDtypeStruct((moved, row_count, width), BF16)
+    own_shape = jax.ShapeDtypeStruct((CAP, row_count, width), BF16)
     meta_shape = jax.ShapeDtypeStruct((HOPS, 8, 128), jnp.int32)
     folded_shape = jax.ShapeDtypeStruct((n_blocks, width), BF16)
 
-    send_k, send_v, meta = pl.pallas_call(
+    own_k, own_v, send_k, send_v, meta = pl.pallas_call(
         functools.partial(pack_kernel, n),
-        out_shape=(moved_shape, moved_shape, meta_shape),
-        in_specs=[smem, smem, smem, hbm, hbm],
-        out_specs=(hbm, hbm, smem),
-        scratch_shapes=[pltpu.SMEM((HOPS,), jnp.int32), pltpu.SemaphoreType.DMA],
+        out_shape=(own_shape, own_shape, moved_shape, moved_shape, meta_shape),
+        in_specs=[smem, smem, smem, vmem, vmem],
+        out_specs=(vmem, vmem, vmem, vmem, smem),
+        scratch_shapes=[pltpu.SMEM((HOPS,), jnp.int32)],
+        compiler_params=pltpu.CompilerParams(vmem_limit_bytes=32 * 2**20),
         name="pack_blocks",
     )(keep_list, dest_slot, blk_req, key_cache, value_cache)
 
     block_rows = pltpu.VMEM((n_blocks, width), F32)
     request_rows = pltpu.VMEM((n, each, width), F32)
+    partials = pltpu.VMEM((n, each, width + 256), F32)
     three_parts = pltpu.VMEM((n, 3, each, width), F32)
     recv_k, recv_v, recv_meta, folded_keys, folded_values, attn_out = pl.pallas_call(
         functools.partial(main_kernel, n, n_heads),
@@ -511,12 +533,12 @@
             three_parts,
             three_parts,
             request_rows,
-            three_parts,
-            three_parts,
+            partials,
+            partials,
             request_rows,
             pltpu.VMEM((n_heads, requests, w_out.shape[1]), F32),
             pltpu.SemaphoreType.DMA((2,)),
-            pltpu.SemaphoreType.DMA((2, 2 * (HOPS - 1))),
+            pltpu.SemaphoreType.DMA((4, (HOPS - 1) * CAP)),
             pltpu.SemaphoreType.DMA((2, HOPS)),
             pltpu.SemaphoreType.DMA((10, n)),
             pltpu.SemaphoreType.DMA((2, n_heads)),
@@ -548,11 +570,12 @@
     packed_keys, packed_values, packed_request = pl.pallas_call(
         place_kernel,
         out_shape=(packed_shape, packed_shape, jax.ShapeDtypeStruct((SLOT_DEV,), jnp.int32)),
-        in_specs=[smem, hbm, hbm, hbm, hbm],
+        in_specs=[smem, vmem, vmem, vmem, vmem],
         out_specs=(hbm, hbm, smem),
         scratch_shapes=[pltpu.VMEM((row_count, width), BF16), pltpu.SemaphoreType.DMA],
+        compiler_params=pltpu.CompilerParams(vmem_limit_bytes=32 * 2**20),
         name="place_blocks",
-    )(recv_meta, key_cache, value_cache, recv_k, recv_v)
+    )(recv_meta, own_k, own_v, recv_k, recv_v)
     return (packed_keys, packed_values, packed_request, folded_keys, folded_values, attn_out)
 
 

time: 343 us -> 126 us (0.37)
  the two profiles are of different devices: /device:TPU:1 before, /device:TPU:0 now
where the time goes in v2:
time: 126 us
  Pallas kernels  113 us (90%)
  local copies, waits for them, and re-layouts  9.1 us (7%)
  other arithmetic  2.84 us (2%)
    pallas_call x1, Pallas kernels, shards(): pl.pallas_call(functools.partial(main_kernel, n, n_heads), out_shape=(mov...  108 us
    unnamed x23, local copies, waits for them, and re-layouts  8.76 us
    pallas_call x1, Pallas kernels, shards(): pl.pallas_call(place_kernel, out_shape=(packed_shape, packed_shape, jax.S...  3.31 us

profile of v2, /device:TPU:0, one launch (start us, length us, event | category | flops | bytes accessed | tf_op | source)
XLA Modules:
  0.0 126.1 jit_solution(2478836674586625287)
XLA Ops:
  0.6 0.7 convert_element_type.18
  1.3 0.8 select_reduce_fusion
  2.1 0.2 convert_reduce_fusion.req
  2.3 0.7 compare_convert_fusion.1
  2.9 0.1 fusion.1.onehot
  3.0 0.2 compare_convert_fusion
  3.2 0.1 broadcast_in_dim.30.keep
  3.3 0.2 fusion.3
  3.5 0.1 pad_maximum_fusion
  3.6 0.1 tile.17.cos
  3.8 0.1 tile.19.sin
  3.9 0.0 copy-start
  3.9 1.7 %copy-done = bf16[18,128,512]{2,1,0:T(8,128)(2,1)S(1)} copy-done((bf16[18,128,512]{2,1,0:T(8,128)(2,1)S(1)}, bf16[18,128,512]{2,1,0:T(8,128)(2,1)}, u32[]{:S(2)}) %copy-start) | copy-done | bytes 2359320
  5.5 0.0 copy-start.1
  5.5 1.7 %copy-done.1 = bf16[18,128,512]{2,1,0:T(8,128)(2,1)S(1)} copy-done((bf16[18,128,512]{2,1,0:T(8,128)(2,1)S(1)}, bf16[18,128,512]{2,1,0:T(8,128)(2,1)}, u32[]{:S(2)}) %copy-start.1) | copy-done | bytes 2359320
  7.2 0.0 copy-start.8
  7.2 0.7 copy-done.8
  7.9 0.0 copy-start.9
  7.9 0.7 copy-done.9
  8.5 2.2 %pack_blocks.1 = (bf16[4,128,512]{2,1,0:T(8,128)(2,1)S(1)}, bf16[4,128,512]{2,1,0:T(8,128)(2,1)S(1)}, bf16[12,128,512]{2,1,0:T(8,128)(2,1)S(1)}, bf16[12,128,512]{2,1,0:T(8,128)(2,1)S(1)}, s32[4,8,128]{2,1,0:T(8,128)S(1)}) custom-call(s32[18]{0:T(128)S(1)} %copy-done.8, s32[18]{0:T(128)S(1)} %copy-done.9, s32[18]{0:T(128)S(1)} %convert_reduce_fusion.req, ...), custom_call_target="tpu_custom_call" | custom-call | tf_op jit(solution)/shard_map/pack_blocks/pallas_call | solution.py:498
  10.7 0.0 copy-start.2
  10.7 1.1 copy-done.2
  11.8 1.1 copy-done.3
  13.0 0.0 copy-done.4
  13.0 0.0 copy-done.5
  13.0 0.0 copy-done.6
  13.0 0.0 copy-done.7
  13.0 107.9 %decode_and_move.1 = (bf16[12,128,512]{2,1,0:T(8,128)(2,1)S(1)}, bf16[12,128,512]{2,1,0:T(8,128)(2,1)S(1)}, s32[4,8,128]{2,1,0:T(8,128)S(1)}, bf16[18,512]{1,0:T...) custom-call(bf16[64,256]{1,0:T(8,128)(2,1)S(1)} %copy-done.6, ...), custom_call_target="tpu_custom_call" | custom-call | tf_op jit(solution)/shard_map/decode_and_move/pallas_call | solution.py:512
  120.9 3.3 %place_blocks.1 = (bf16[16,128,512]{2,1,0:T(8,128)(2,1)}, bf16[16,128,512]{2,1,0:T(8,128)(2,1)}, s32[16]{0:T(128)}) custom-call(s32[4,8,128]{2,1,0:T(8,128)S(1)} %get-tuple-element.23.meta, bf16[4,128,512]{2,1,0:T(8,128)(2,1)S(1)} %get-tuple-element.24.own_k, bf16[4,128,512]{2,1,0:T(8,128)(2,1)S(1)} %get-tuple-element.25.own_v, ...), custom_call_target="tpu_custom_call" | custom-call | tf_op jit(solution)/shard_map/place_blocks/pallas_call | solution.py:570
  124.2 0.6 copy.19
  124.8 0.6 copy.20
  125.4 0.6 copy.21
  (11 shorter events, 0.1 us)
Async XLA Ops:
  3.9 1.7 %copy-start = (bf16[18,128,512]{2,1,0:T(8,128)(2,1)S(1)}, bf16[18,128,512]{2,1,0:T(8,128)(2,1)}, u32[]{:S(2)}) copy-start(bf16[18,128,512]{2,1,0:T(8,128)(2,1)} %keys.3) | copy-start | bytes 7077892
  5.5 1.7 %copy-start.1 = (bf16[18,128,512]{2,1,0:T(8,128)(2,1)S(1)}, bf16[18,128,512]{2,1,0:T(8,128)(2,1)}, u32[]{:S(2)}) copy-start(bf16[18,128,512]{2,1,0:T(8,128)(2,1)} %values.3) | copy-start | bytes 7077892
  7.2 0.7 copy-start.8
  7.9 0.7 copy-start.9
  8.5 4.5 %copy-start.4 = (bf16[256,3,512]{2,0,1:T(8,128)(2,1)S(1)}, bf16[256,3,512]{2,0,1:T(8,128)(2,1)}, u32[]{:S(2)}) copy-start(bf16[256,3,512]{2,0,1:T(8,128)(2,1)} %param.11) | copy-start | bytes 2359300
  8.5 4.5 %copy-start.5 = (bf16[512,256]{1,0:T(8,128)(2,1)S(1)}, bf16[512,256]{1,0:T(8,128)(2,1)}, u32[]{:S(2)}) copy-start(bf16[512,256]{1,0:T(8,128)(2,1)} %w_out.1) | copy-start | bytes 786436
  8.5 4.5 %copy-start.6 = (bf16[64,256]{1,0:T(8,128)(2,1)S(1)}, bf16[64,256]{1,0:T(8,128)(2,1)}, u32[]{:S(2)}) copy-start(bf16[64,256]{1,0:T(8,128)(2,1)} %hidden.1) | copy-start | bytes 98308
  8.5 4.5 %copy-start.7 = (f32[18,128]{1,0:T(8,128)S(1)}, f32[18,128]{1,0:T(8,128)}, u32[]{:S(2)}) copy-start(f32[18,128]{1,0:T(8,128)} %fold_w.1) | copy-start | bytes 27652
  10.7 1.1 copy-start.2
  11.8 1.1 copy-start.3
